TPU v7x, 32 devices: a whole 2x2x4 slice. The times are simulated.
32 devices in a mesh: groups: 2 (over x), dp: 16 (over z, y, core).
Axes of the slice: x: 2, y: 2, z: 4, core: 2. Of those that a mesh axis runs over, the one named last changes fastest.
Arguments:
- test_feats: bfloat16 [1024, 8192], P('groups', 'dp'), parts along dimension 0, may hold values from -6 to 6
- precond: bfloat16 [8192, 8192], P('dp'), may hold values from -0.0625 to 0.0625
- train_feats: bfloat16 [16384, 8192], P(('groups', 'dp')), parts along dimension 0, may hold values from -6 to 6
- train_prob: float32 [16384], P(('groups', 'dp')), parts along dimension 0, may hold values from 0.05 to 0.95
Outputs:
- scores: float32 [16384, 512], P(('groups', 'dp')), parts along dimension 0
There are 2 independent parts, one for each index of `groups`. A program takes and returns all parts, laid end to end along the dimension named above; an argument that names none is the same for every part. Nothing has to cross between parts.
All inputs are finite; a program needn't handle non-finite values.
Results may differ from a plain program's by a relative error of at most 0.0029.
Values may be sent and summed in bfloat16 or wider, within the bound.
A program may use at most 128 MiB of HBM per device.

v0:
```python
import jax
import jax.numpy as jnp
from jax import lax
from jax.sharding import PartitionSpec as P


def make_fold(train_feats):

    def accumulate(total, piece, start):
        return jnp.dot(train_feats, piece, preferred_element_type=jnp.float32)

    return accumulate


def per_device(test_feats, precond, train_feats, train_prob):
    accumulate = make_fold(train_feats)
    empty = jnp.zeros((train_feats.shape[0], test_feats.shape[0]), jnp.float32)
    own_rows = lax.psum_scatter(
        lax.dot_general(
            precond, test_feats, (((0,), (1,)), ((), ())), preferred_element_type=jnp.float32
        ),
        "dp",
        scatter_dimension=0,
        tiled=True,
    ).astype(jnp.bfloat16)
    raw_scores = accumulate(empty, lax.all_gather(own_rows, "dp", axis=0, tiled=True), jnp.int32(0))
    return raw_scores * (1.0 - train_prob)[:, None]


def solution(mesh):
    return jax.shard_map(
        per_device,
        mesh=mesh,
        in_specs=(P("groups", "dp"), P("dp", None), P(("groups", "dp"), None), P(("groups", "dp"))),
        out_specs=P(("groups", "dp"), None),
        check_vma=False,
    )
```

profile of v0, /device:TPU:0, one launch (start us, length us, event | category | flops | bytes accessed | tf_op | source)
XLA Modules:
  0.0 294.6 jit_solution(14682580135946347539)
XLA Ops:
  6.5 0.0 copy-start
  6.5 0.0 reduce-scatter.2.cloned.1.call-start
  6.5 1.0 copy-done
  7.6 11.7 %fusion.1 = f32[8192,512]{1,0:T(8,128)} fusion(bf16[512,8192]{1,0:T(8,128)(2,1)} %param.5, bf16[512,512]{1,0:T(8,128)(2,1)S(1)} %copy-done), kind=kOutput, calls=%fused_computation.3 | convolution fusion | flops 4294967296 | bytes 25690112 | tf_op jit(solution)/shard_map/dot_general | solution.py:19
  19.2 0.0 copy-start.1
  19.2 0.0 reduce-scatter.2.cloned.1.call-update
  19.3 0.0 all-gather.2.cloned.1.call-start
  19.3 181.3 %reduce-scatter.2.cloned.1.call-done = f32[512,512]{1,0:T(8,128)} async-done(((f32[8192,512]{1,0:T(8,128)}), f32[512,512]{1,0:T(8,128)}) %reduce-scatter.2.cloned.1.call-update) | async-done | bytes 1048592 | tf_op jit(solution)/shard_map/reduce_scatter | solution.py:18
  200.7 2.1 convert_element_type.3
  202.8 0.0 all-gather.2.cloned.1.call-update
  202.8 0.0 copy-done.1
  202.8 74.1 %all-gather.2.cloned.1.call-done = bf16[8192,512]{1,0:T(8,128)(2,1)} async-done(((bf16[512,512]{1,0:T(8,128)(2,1)}), bf16[8192,512]{1,0:T(8,128)(2,1)}) %all-gather.2.cloned.1.call-update) | async-done | bytes 8388624 | tf_op jit(solution)/shard_map/all_gather | solution.py:26
  276.9 9.5 %fusion = f32[512,512]{0,1:T(8,128)S(1)} fusion(bf16[8192,512]{1,0:T(8,128)(2,1)} %all-gather.2.cloned.1.call-done, bf16[512,8192]{1,0:T(8,128)(2,1)} %param.6, f32[512]{0:T(512)S(1)} %broadcast_subtract_fusion), kind=kOutput, calls=%fused_computation.1 | convolution fusion | flops 4295229440 | bytes 17827840 | tf_op jit(solution)/shard_map/dot_general | solution.py:10
  286.4 1.3 copy.5
  (1 shorter events, 0.0 us)
Async XLA Ops:
  6.5 1.0 copy-start
  6.5 194.1 %reduce-scatter.2.cloned.1.call-start = ((), (), s32[]{:S(2)}) async-start(), calls=%async_computation.1 | async-start | bytes 17825792 | tf_op jit(solution)/shard_map/reduce_scatter | solution.py:18
  19.2 183.5 %copy-start.1 = (f32[512]{0:T(512)S(1)}, f32[512]{0:T(512)}, u32[]{:S(2)}) copy-start(f32[512]{0:T(512)} %param.7) | copy-start | bytes 6148
  19.3 257.6 %all-gather.2.cloned.1.call-start = ((), (), s32[]{:S(2)}) async-start(), calls=%async_computation.2 | async-start | bytes 8912896 | tf_op jit(solution)/shard_map/all_gather | solution.py:26
Sparse Core Ops, SparseCore 0:
  19.4 181.2 reduce-scatter.1
  202.9 73.9 all-gather.1
where the time goes:
time: 295 us
  waiting for transfers between devices  255 us (86%)
  matrix products  21.2 us (7%)
  between operations  13.4 us (5%)
    reduce_scatter x1, waiting for transfers between devices, per_device(): lax.psum_scatter(lax.dot_general(precond, test_feats, (((0,), (1,)), ((),...  181 us
    all_gather x1, waiting for transfers between devices, per_device(): lax.all_gather(own_rows, 'dp', axis=0, tiled=True)  74.1 us
    dot_general x1, matrix products, per_device(): lax.dot_general(precond, test_feats, (((0,), (1,)), ((), ())), preferred_...  11.7 us
    dot_general x1, matrix products, accumulate(): return jnp.dot(train_feats, piece, preferred_element_type=jnp.float32)  9.55 us
  transfers between devices with their start and end apart: 2, of which 2 were waited for; matrix products, arithmetic and copies ran while one was open for 0% of the time, Pallas kernels for 0%

commit v1 on v0

v1 whole, which is shorter than its diff:
```python
import functools

import jax
import jax.numpy as jnp
from jax import lax
from jax.experimental import pallas as pl
from jax.experimental.pallas import tpu as pltpu
from jax.sharding import PartitionSpec as P

MESH = pl.DeviceIdType.MESH
F32, BF16 = jnp.float32, jnp.bfloat16


def narrow_hops(chips):
    count = 0
    while (count + 1) * (count + 2) <= 0.8 * chips and count + 1 < chips // 2:
        count += 1
    return count


def kernel(
    chips, folded, narrow,
    test_ref, precond_hbm, train_hbm, out_ref,
    test_other, own_p, other_p, train, part, mine,
    send16, send32, recv16, recv32, gathered,
    test_sems, own_sems, other_sems, train_sem,
    ring_sems, spread_sems, pair_sems,
):
    half = chips // 2
    tests, depth = test_ref.shape
    rows = tests // 2
    feats = own_p.shape[2]
    index = lax.axis_index("dp")
    core = index % 2
    chip = index // 2
    if folded:
        pos = chip // 2 + (chip % 2) * (chips - 1 - 2 * (chip // 2))
    else:
        pos = chip

    def device(place):
        place = (place + chips) % chips
        if folded:
            side = place // half
            place = 2 * (place + side * (chips - 1 - 2 * place)) + side
        return {"dp": place * 2 + core}

    pair = {"dp": chip * 2 + 1 - core}
    towards = (device(pos + 1), device(pos - 1))

    def columns(offset, which):
        block = ((pos + offset + chips) % chips) * 2 + which
        return pl.ds(pl.multiple_of(block * feats, feats), feats)

    order = [half]
    for distance in range(half - 1, 0, -1):
        order += [distance, -distance]
    order.append(0)

    barrier = pltpu.get_barrier_semaphore()
    train_copy = pltpu.make_async_copy(train_hbm, train, train_sem)
    own_copies = [
        pltpu.make_async_copy(
            precond_hbm.at[:, columns(offset, core)], own_p.at[at], own_sems.at[at]
        )
        for at, offset in enumerate(order)
    ]
    for copy in own_copies:
        copy.start()
    for other in (pair, *towards):
        pl.semaphore_signal(barrier, inc=1, device_id=other, device_id_type=MESH)
    pl.semaphore_wait(barrier, 3)

    def remote(src, dst, sems, where):
        return pltpu.make_async_remote_copy(
            src_ref=src, dst_ref=dst,
            send_sem=sems.at[(0, *where)], recv_sem=sems.at[(1, *where)],
            device_id=where_to[0], device_id_type=MESH,
        )

    where_to = [pair]
    sent = []
    test_copy = remote(test_ref, test_other, test_sems, (0,))
    test_copy.start()
    sent.append(test_copy)
    other_copies = []
    for at, offset in enumerate(order):
        copy = remote(
            precond_hbm.at[:, columns(offset, 1 - core)], other_p.at[at], other_sems, (at,)
        )
        copy.start()
        sent.append(copy)
        other_copies.append(copy)
    train_copy.start()

    tile = min(rows, 256)

    def partial_sum(offset, target):
        at = order.index(offset)
        own_copies[at].wait()
        if at == 0:
            test_copy.wait_recv()
        other_copies[at].wait_recv()

        @pl.loop(0, tests // tile)
        def _(step):
            here = pl.ds(pl.multiple_of(step * tile, tile), tile)
            target[here, :] = jnp.dot(
                test_ref[here, :], own_p[at], preferred_element_type=F32
            ) + jnp.dot(test_other[here, :], other_p[at], preferred_element_type=F32)

    def slot(way, which, step):
        count = step + 1 if way == which else step
        if count <= narrow:
            return send16.at[way, which, step], recv16.at[way, which, step]
        return send32.at[way, which, step - narrow], recv32.at[way, which, step - narrow]

    ring = {}
    sign = (1, -1)
    partial_sum(half, part.at[0])
    for step in range(half):
        if step > 0:
            for way in (0, 1):
                partial_sum(sign[way] * (half - step), part.at[way])
        for leg in (0, 1):
            for way in (0, 1):
                which = way if leg == 0 else 1 - way
                if step == 0 and leg == 1:
                    continue
                source, target = slot(way, which, step)
                value = part[0 if step == 0 else way, pl.ds(which * rows, rows), :]
                if (way, which, step - 1) in ring:
                    ring[way, which, step - 1].wait_recv()
                    value = value + slot(way, which, step - 1)[1][...].astype(F32)
                source[...] = value.astype(source.dtype)
                where_to[0] = towards[way]
                copy = remote(source, target, ring_sems, (way, which, step))
                copy.start()
                sent.append(copy)
                ring[way, which, step] = copy
    partial_sum(0, mine)

    def place(offset, which):
        return ((pos + offset + chips) % chips) * 2 + which

    def span(which):
        return pl.ds(which * rows, rows)

    spread, paired = {}, {}

    def forward(way, which, step):
        block = gathered.at[place(-sign[way] * step, core), span(which)]
        where_to[0] = towards[way]
        copy = remote(block, block, spread_sems, (way, which, step))
        copy.start()
        sent.append(copy)
        spread[way, which, step] = copy

    def hand_over(way, which, step):
        block = gathered.at[place(-sign[way] * step, core), span(which)]
        where_to[0] = pair
        copy = remote(block, block, pair_sems, (way, which, step))
        copy.start()
        sent.append(copy)
        paired[way, which, step] = copy

    out_ref[...] = jnp.zeros_like(out_ref)

    def fold(offset, owner, which):
        block = place(offset, owner)
        cols = pl.ds(pl.multiple_of(block * feats, feats), feats)
        size = min(256, out_ref.shape[0])

        @pl.loop(0, out_ref.shape[0] // size)
        def _(step):
            here = pl.ds(pl.multiple_of(step * size, size), size)
            out_ref[here, which * rows:(which + 1) * rows] += lax.dot_general(
                train[here, cols], gathered[block, span(which), :],
                (((1,), (1,)), ((), ())), preferred_element_type=F32,
            )

    train_copy.wait()
    ready = []
    for which in (0, 1):
        total = mine[span(which), :]
        for way in (0, 1):
            ring[way, which, half - 1].wait_recv()
            total = total + slot(way, which, half - 1)[1][...].astype(F32)
        gathered[place(0, core), span(which), :] = total.astype(BF16)
        for way in (0, 1):
            if half > 1 or way == which:
                forward(way, which, 0)
        hand_over(0, which, 0)
        ready += [(0, core, which, None), (0, 1 - core, which, (0, which, 0))]

    def drain(limit):
        while len(ready) > limit:
            offset, owner, which, key = ready.pop(0)
            if key is not None:
                paired[key].wait_recv()
            fold(offset, owner, which)

    for step in range(1, half + 1):
        for which in (0, 1):
            for way in (0, 1):
                if (way, which, step - 1) not in spread:
                    continue
                spread[way, which, step - 1].wait_recv()
                if step < half and (step + 1 < half or way == which):
                    forward(way, which, step)
                hand_over(way, which, step)
                offset = -sign[way] * step
                ready += [
                    (offset, core, which, None), (offset, 1 - core, which, (way, which, step))
                ]
            drain(4)
    drain(0)
    for copy in sent:
        copy.wait_send()


def per_device(chips, test_feats, precond, train_feats, train_prob):
    tests, depth = test_feats.shape
    features = precond.shape[1]
    feats = features // (2 * chips)
    rows, half = tests // 2, chips // 2
    narrow = narrow_hops(chips)
    wide = half - narrow
    trains = train_feats.shape[0]
    dma = pltpu.SemaphoreType.DMA
    raw_scores = pl.pallas_call(
        functools.partial(kernel, chips, chips <= 8, narrow),
        out_shape=jax.ShapeDtypeStruct((trains, tests), F32),
        in_specs=[
            pl.BlockSpec(memory_space=pltpu.VMEM),
            pl.BlockSpec(memory_space=pl.ANY),
            pl.BlockSpec(memory_space=pl.ANY),
        ],
        out_specs=pl.BlockSpec(memory_space=pltpu.VMEM),
        scratch_shapes=[
            pltpu.VMEM((tests, depth), BF16),
            pltpu.VMEM((chips, depth, feats), BF16),
            pltpu.VMEM((chips, depth, feats), BF16),
            pltpu.VMEM((trains, features), BF16),
            pltpu.VMEM((2, tests, feats), F32),
            pltpu.VMEM((tests, feats), F32),
            pltpu.VMEM((2, 2, narrow + 1, rows, feats), BF16),
            pltpu.VMEM((2, 2, wide, rows, feats), F32),
            pltpu.VMEM((2, 2, narrow + 1, rows, feats), BF16),
            pltpu.VMEM((2, 2, wide, rows, feats), F32),
            pltpu.VMEM((2 * chips, tests, feats), BF16),
            dma((2, 1)),
            dma((chips,)),
            dma((2, chips)),
            dma,
            dma((2, 2, 2, half)),
            dma((2, 2, 2, half)),
            dma((2, 2, 2, half + 1)),
        ],
        compiler_params=pltpu.CompilerParams(
            collective_id=0, has_side_effects=True, vmem_limit_bytes=56 * 2**20
        ),
        cost_estimate=pl.CostEstimate(
            flops=4 * tests * depth * features + 2 * trains * tests * features,
            bytes_accessed=2 * (depth + trains) * features + 4 * trains * tests,
            transcendentals=0,
        ),
    )(test_feats, precond, train_feats)
    return raw_scores * (1.0 - train_prob)[:, None]


def solution(mesh):
    return jax.shard_map(
        functools.partial(per_device, mesh.shape["dp"] // 2),
        mesh=mesh,
        in_specs=(P("groups", "dp"), P("dp", None), P(("groups", "dp"), None), P(("groups", "dp"))),
        out_specs=P(("groups", "dp"), None),
        check_vma=False,
    )
```

time: 295 us -> 119 us (0.40)
  waiting for transfers between devices: 255 us -> 0 us
  Pallas kernels: 0 us -> 116 us
  matrix products: 21.2 us -> 0 us
  between operations: 13.4 us -> 0.01 us
    reduce_scatter x1 -> x0, waiting for transfers between devices: 181 us -> none  [per_device(): lax.psum_scatter(lax.dot_general(precond, test_feats, (((0,), (1,)), ((),...]
    pallas_call x0 -> x1, Pallas kernels: none -> 116 us  [per_device(): pl.pallas_call(functools.partial(kernel, chips, chips <= 8, narrow), out_...]
    all_gather x1 -> x0, waiting for transfers between devices: 74.1 us -> none  [per_device(): lax.all_gather(own_rows, 'dp', axis=0, tiled=True)]
    dot_general x2 -> x0, matrix products: 21.2 us -> none  [the longest x1 11.7 us: per_device(): lax.dot_general(precond, test_feats, (((0,), (1,)), ((), ())), preferred_...]
  transfers between devices with their start and end apart: 2 -> 0, of which waited for: 2 -> 0; matrix products, arithmetic and copies ran while one was open for 0% -> 0% of each run, Pallas kernels for 0% -> 0%
where the time goes in v1:
time: 119 us
  Pallas kernels  116 us (97%)
  other arithmetic  3.01 us (3%)
    pallas_call x1, Pallas kernels, per_device(): pl.pallas_call(functools.partial(kernel, chips, chips <= 8, narrow), out_...  116 us

profile of v1, /device:TPU:0, one launch (start us, length us, event | category | flops | bytes accessed | tf_op | source)
XLA Modules:
  0.0 118.7 jit_solution(2331612909924165977)
XLA Ops:
  0.0 0.7 broadcast_subtract_fusion
  0.7 115.7 %shard_map.46 = f32[512,512]{1,0:T(8,128)} custom-call(bf16[512,512]{1,0:T(8,128)(2,1)} %test_ref.1, bf16[512,8192]{1,0:T(8,128)(2,1)} %precond_hbm.1, bf16[512,8192]{1,0:T(8,128)(2,1)} %train_hbm.1), custom_call_target="tpu_custom_call" | custom-call | flops 12884901888 | bytes 17825792 | tf_op jit(solution)/shard_map/pallas_call | solution.py:231
  116.3 2.3 %broadcast_multiply_fusion = f32[512,512]{1,0:T(8,128)} fusion(f32[512,512]{1,0:T(8,128)} %shard_map.46, f32[512]{0:T(512)S(1)} %broadcast_subtract_fusion), kind=kLoop, calls=%fused_computation | loop fusion | flops 262144 | bytes 2099200 | tf_op jit(solution)/shard_map/mul | solution.py:269

commit v2 on v1

--- a/solution.py
+++ b/solution.py
@@ -8,6 +8,8 @@
 from jax.sharding import PartitionSpec as P
 
 MESH = pl.DeviceIdType.MESH
+SUBS = 2
+AHEAD = 3
 F32, BF16 = jnp.float32, jnp.bfloat16
 
 
@@ -29,6 +31,7 @@
     half = chips // 2
     tests, depth = test_ref.shape
     rows = tests // 2
+    piece = rows // SUBS
     feats = own_p.shape[2]
     index = lax.axis_index("dp")
     core = index % 2
@@ -65,7 +68,7 @@
         )
         for at, offset in enumerate(order)
     ]
-    for copy in own_copies:
+    for copy in own_copies[:AHEAD]:
         copy.start()
     for other in (pair, *towards):
         pl.semaphore_signal(barrier, inc=1, device_id=other, device_id_type=MESH)
@@ -88,10 +91,10 @@
         copy = remote(
             precond_hbm.at[:, columns(offset, 1 - core)], other_p.at[at], other_sems, (at,)
         )
-        copy.start()
         sent.append(copy)
         other_copies.append(copy)
-    train_copy.start()
+    for copy in other_copies[:AHEAD]:
+        copy.start()
 
     tile = min(rows, 256)
 
@@ -109,11 +112,14 @@
                 test_ref[here, :], own_p[at], preferred_element_type=F32
             ) + jnp.dot(test_other[here, :], other_p[at], preferred_element_type=F32)
 
-    def slot(way, which, step):
-        count = step + 1 if way == which else step
+    def slot(way, part_at, step):
+        count = step + 1 if way == part_at // SUBS else step
         if count <= narrow:
-            return send16.at[way, which, step], recv16.at[way, which, step]
-        return send32.at[way, which, step - narrow], recv32.at[way, which, step - narrow]
+            return send16.at[way, part_at, step], recv16.at[way, part_at, step]
+        return send32.at[way, part_at, step - narrow], recv32.at[way, part_at, step - narrow]
+
+    def span(part_at):
+        return pl.ds(part_at * piece, piece)
 
     ring = {}
     sign = (1, -1)
@@ -122,29 +128,31 @@
         if step > 0:
             for way in (0, 1):
                 partial_sum(sign[way] * (half - step), part.at[way])
-        for leg in (0, 1):
-            for way in (0, 1):
-                which = way if leg == 0 else 1 - way
-                if step == 0 and leg == 1:
-                    continue
-                source, target = slot(way, which, step)
-                value = part[0 if step == 0 else way, pl.ds(which * rows, rows), :]
-                if (way, which, step - 1) in ring:
-                    ring[way, which, step - 1].wait_recv()
-                    value = value + slot(way, which, step - 1)[1][...].astype(F32)
-                source[...] = value.astype(source.dtype)
-                where_to[0] = towards[way]
-                copy = remote(source, target, ring_sems, (way, which, step))
+        for leg in (0,) if step == 0 else (1, 0):
+            for sub in range(SUBS):
+                for way in (0, 1):
+                    at = (way if leg == 0 else 1 - way) * SUBS + sub
+                    source, target = slot(way, at, step)
+                    value = part[0 if step == 0 else way, span(at), :]
+                    if (way, at, step - 1) in ring:
+                        ring[way, at, step - 1].wait_recv()
+                        value = value + slot(way, at, step - 1)[1][...].astype(F32)
+                    source[...] = value.astype(source.dtype)
+                    where_to[0] = towards[way]
+                    copy = remote(source, target, ring_sems, (way, at, step))
+                    copy.start()
+                    sent.append(copy)
+                    ring[way, at, step] = copy
+        if step == 0:
+            for copy in own_copies[AHEAD:] + other_copies[AHEAD:]:
                 copy.start()
-                sent.append(copy)
-                ring[way, which, step] = copy
+            out_ref[...] = jnp.zeros_like(out_ref)
+        if step == min(1, half - 1):
+            train_copy.start()
     partial_sum(0, mine)
 
     def place(offset, which):
         return ((pos + offset + chips) % chips) * 2 + which
-
-    def span(which):
-        return pl.ds(which * rows, rows)
 
     spread, paired = {}, {}
 
@@ -164,8 +172,6 @@
         sent.append(copy)
         paired[way, which, step] = copy
 
-    out_ref[...] = jnp.zeros_like(out_ref)
-
     def fold(offset, owner, which):
         block = place(offset, owner)
         cols = pl.ds(pl.multiple_of(block * feats, feats), feats)
@@ -175,44 +181,49 @@
         def _(step):
             here = pl.ds(pl.multiple_of(step * size, size), size)
             out_ref[here, which * rows:(which + 1) * rows] += lax.dot_general(
-                train[here, cols], gathered[block, span(which), :],
+                train[here, cols], gathered[block, pl.ds(which * rows, rows), :],
                 (((1,), (1,)), ((), ())), preferred_element_type=F32,
             )
 
     train_copy.wait()
     ready = []
-    for which in (0, 1):
-        total = mine[span(which), :]
+    parts = [which * SUBS + sub for sub in range(SUBS) for which in (0, 1)]
+
+    def arrived(offset, way, at, step):
+        which, sub = at // SUBS, at % SUBS
+        if sub == SUBS - 1:
+            keys = [(way, which * SUBS + k, step) for k in range(SUBS)]
+            ready.extend([(offset, core, which, []), (offset, 1 - core, which, keys)])
+
+    for at in parts:
+        total = mine[span(at), :]
         for way in (0, 1):
-            ring[way, which, half - 1].wait_recv()
-            total = total + slot(way, which, half - 1)[1][...].astype(F32)
-        gathered[place(0, core), span(which), :] = total.astype(BF16)
+            ring[way, at, half - 1].wait_recv()
+            total = total + slot(way, at, half - 1)[1][...].astype(F32)
+        gathered[place(0, core), span(at), :] = total.astype(BF16)
         for way in (0, 1):
-            if half > 1 or way == which:
-                forward(way, which, 0)
-        hand_over(0, which, 0)
-        ready += [(0, core, which, None), (0, 1 - core, which, (0, which, 0))]
+            if half > 1 or way == at // SUBS:
+                forward(way, at, 0)
+        hand_over(0, at, 0)
+        arrived(0, 0, at, 0)
 
     def drain(limit):
         while len(ready) > limit:
-            offset, owner, which, key = ready.pop(0)
-            if key is not None:
+            offset, owner, which, keys = ready.pop(0)
+            for key in keys:
                 paired[key].wait_recv()
             fold(offset, owner, which)
 
     for step in range(1, half + 1):
-        for which in (0, 1):
+        for at in parts:
             for way in (0, 1):
-                if (way, which, step - 1) not in spread:
+                if (way, at, step - 1) not in spread:
                     continue
-                spread[way, which, step - 1].wait_recv()
-                if step < half and (step + 1 < half or way == which):
-                    forward(way, which, step)
-                hand_over(way, which, step)
-                offset = -sign[way] * step
-                ready += [
-                    (offset, core, which, None), (offset, 1 - core, which, (way, which, step))
-                ]
+                spread[way, at, step - 1].wait_recv()
+                if step < half and (step + 1 < half or way == at // SUBS):
+                    forward(way, at, step)
+                hand_over(way, at, step)
+                arrived(-sign[way] * step, way, at, step)
             drain(4)
     drain(0)
     for copy in sent:
@@ -223,7 +234,8 @@
     tests, depth = test_feats.shape
     features = precond.shape[1]
     feats = features // (2 * chips)
-    rows, half = tests // 2, chips // 2
+    pieces, half = 2 * SUBS, chips // 2
+    piece = tests // pieces
     narrow = narrow_hops(chips)
     wide = half - narrow
     trains = train_feats.shape[0]
@@ -244,18 +256,18 @@
             pltpu.VMEM((trains, features), BF16),
             pltpu.VMEM((2, tests, feats), F32),
             pltpu.VMEM((tests, feats), F32),
-            pltpu.VMEM((2, 2, narrow + 1, rows, feats), BF16),
-            pltpu.VMEM((2, 2, wide, rows, feats), F32),
-            pltpu.VMEM((2, 2, narrow + 1, rows, feats), BF16),
-            pltpu.VMEM((2, 2, wide, rows, feats), F32),
+            pltpu.VMEM((2, pieces, narrow + 1, piece, feats), BF16),
+            pltpu.VMEM((2, pieces, wide, piece, feats), F32),
+            pltpu.VMEM((2, pieces, narrow + 1, piece, feats), BF16),
+            pltpu.VMEM((2, pieces, wide, piece, feats), F32),
             pltpu.VMEM((2 * chips, tests, feats), BF16),
             dma((2, 1)),
             dma((chips,)),
             dma((2, chips)),
             dma,
-            dma((2, 2, 2, half)),
-            dma((2, 2, 2, half)),
-            dma((2, 2, 2, half + 1)),
+            dma((2, 2, pieces, half)),
+            dma((2, 2, pieces, half)),
+            dma((2, 2, pieces, half + 1)),
         ],
         compiler_params=pltpu.CompilerParams(
             collective_id=0, has_side_effects=True, vmem_limit_bytes=56 * 2**20

time: 119 us -> 116 us (0.975)
  Pallas kernels: 116 us -> 113 us
    pallas_call x1, Pallas kernels: 116 us -> 113 us  [per_device(): pl.pallas_call(functools.partial(kernel, chips, chips <= 8, narrow), out_...]
where the time goes in v2:
time: 116 us
  Pallas kernels  113 us (97%)
  other arithmetic  3.01 us (3%)
    pallas_call x1, Pallas kernels, per_device(): pl.pallas_call(functools.partial(kernel, chips, chips <= 8, narrow), out_...  113 us
    mul x1, other arithmetic, per_device(): return raw_scores * (1.0 - train_prob)[:, None]  2.33 us

profile of v2, /device:TPU:0, one launch (start us, length us, event | category | flops | bytes accessed | tf_op | source)
XLA Modules:
  0.0 115.7 jit_solution(8389019695126309805)
XLA Ops:
  0.0 0.7 broadcast_subtract_fusion
  0.7 112.7 %shard_map.46 = f32[512,512]{1,0:T(8,128)} custom-call(bf16[512,512]{1,0:T(8,128)(2,1)} %test_ref.1, bf16[512,8192]{1,0:T(8,128)(2,1)} %precond_hbm.1, bf16[512,8192]{1,0:T(8,128)(2,1)} %train_hbm.1), custom_call_target="tpu_custom_call" | custom-call | flops 12884901888 | bytes 17825792 | tf_op jit(solution)/shard_map/pallas_call | solution.py:243
  113.4 2.3 %broadcast_multiply_fusion = f32[512,512]{1,0:T(8,128)} fusion(f32[512,512]{1,0:T(8,128)} %shard_map.46, f32[512]{0:T(512)S(1)} %broadcast_subtract_fusion), kind=kLoop, calls=%fused_computation | loop fusion | flops 262144 | bytes 2099200 | tf_op jit(solution)/shard_map/mul | solution.py:281

commit v3 on v2

--- a/solution.py
+++ b/solution.py
@@ -15,7 +15,7 @@
 
 def narrow_hops(chips):
     count = 0
-    while (count + 1) * (count + 2) <= 0.8 * chips and count + 1 < chips // 2:
+    while (count + 2) ** 2 <= 1.125 * chips and count + 1 < chips // 2:
         count += 1
     return count
 
@@ -113,8 +113,8 @@
             ) + jnp.dot(test_other[here, :], other_p[at], preferred_element_type=F32)
 
     def slot(way, part_at, step):
-        count = step + 1 if way == part_at // SUBS else step
-        if count <= narrow:
+        longer = way == part_at // SUBS
+        if step < narrow if longer else step <= narrow + 1:
             return send16.at[way, part_at, step], recv16.at[way, part_at, step]
         return send32.at[way, part_at, step - narrow], recv32.at[way, part_at, step - narrow]
 
@@ -256,9 +256,9 @@
             pltpu.VMEM((trains, features), BF16),
             pltpu.VMEM((2, tests, feats), F32),
             pltpu.VMEM((tests, feats), F32),
-            pltpu.VMEM((2, pieces, narrow + 1, piece, feats), BF16),
+            pltpu.VMEM((2, pieces, narrow + 2, piece, feats), BF16),
             pltpu.VMEM((2, pieces, wide, piece, feats), F32),
-            pltpu.VMEM((2, pieces, narrow + 1, piece, feats), BF16),
+            pltpu.VMEM((2, pieces, narrow + 2, piece, feats), BF16),
             pltpu.VMEM((2, pieces, wide, piece, feats), F32),
             pltpu.VMEM((2 * chips, tests, feats), BF16),
             dma((2, 1)),

time: 116 us -> 110 us (0.948)
  Pallas kernels: 113 us -> 107 us
    pallas_call x1, Pallas kernels: 113 us -> 107 us  [per_device(): pl.pallas_call(functools.partial(kernel, chips, chips <= 8, narrow), out_...]
where the time goes in v3:
time: 110 us
  Pallas kernels  107 us (97%)
  other arithmetic  3.01 us (3%)
    pallas_call x1, Pallas kernels, per_device(): pl.pallas_call(functools.partial(kernel, chips, chips <= 8, narrow), out_...  107 us
    mul x1, other arithmetic, per_device(): return raw_scores * (1.0 - train_prob)[:, None]  2.33 us

profile of v3, /device:TPU:0, one launch (start us, length us, event | category | flops | bytes accessed | tf_op | source)
XLA Modules:
  0.0 110.1 jit_solution(50155462927382820)
XLA Ops:
  0.0 0.7 broadcast_subtract_fusion
  0.7 107.1 %shard_map.46 = f32[512,512]{1,0:T(8,128)} custom-call(bf16[512,512]{1,0:T(8,128)(2,1)} %test_ref.1, bf16[512,8192]{1,0:T(8,128)(2,1)} %precond_hbm.1, bf16[512,8192]{1,0:T(8,128)(2,1)} %train_hbm.1), custom_call_target="tpu_custom_call" | custom-call | flops 12884901888 | bytes 17825792 | tf_op jit(solution)/shard_map/pallas_call | solution.py:243
  107.8 2.3 %broadcast_multiply_fusion = f32[512,512]{1,0:T(8,128)} fusion(f32[512,512]{1,0:T(8,128)} %shard_map.46, f32[512]{0:T(512)S(1)} %broadcast_subtract_fusion), kind=kLoop, calls=%fused_computation | loop fusion | flops 262144 | bytes 2099200 | tf_op jit(solution)/shard_map/mul | solution.py:281
